TPU v7x, 32 devices: a whole 2x2x4 slice. The times are simulated.
32 devices in a mesh: chan: 16 (over z, x, core), inp: 2 (over y).
Axes of the slice: x: 2, y: 2, z: 4, core: 2. Of those that a mesh axis runs over, the one named last changes fastest.
Arguments:
- voltages: bfloat16 [512, 2, 65536], P('inp', None, 'chan'), may hold values from -64 to 64
Outputs:
- delays: float32 [512, 512, 2, 512], P('inp', 'chan')
All inputs are finite; a program needn't handle non-finite values.
Results may differ from a plain program's by a relative error of at most 0.0053.
Values may be sent and summed in bfloat16 or wider, within the bound.
A program may use at most 192 MiB of HBM per device.

v0:
```python
import math

import jax
import jax.numpy as jnp
from jax import lax
from jax.sharding import PartitionSpec as P

NCH = 512


def taper_weights(count):
    position = jnp.arange(count, dtype=jnp.float32)
    return 0.5 - 0.5 * jnp.cos(2.0 * math.pi * (position + 0.5) / count)


def channel_table(count):
    indices = jnp.arange(count, dtype=jnp.int32)
    product = indices[:, None] * indices[None, :] % count
    angle = 2.0 * math.pi / count * product.astype(jnp.float32)
    window = taper_weights(count)[:, None] / math.sqrt(count)
    cosine = window * jnp.cos(angle)
    sine = window * jnp.sin(angle)
    upper = jnp.concatenate([cosine, -sine], axis=1)
    lower = jnp.concatenate([sine, cosine], axis=1)
    return jnp.concatenate([upper, lower], axis=0).astype(jnp.bfloat16)


def dft_tables(row_count, col_count, modulus):
    row_idx = jnp.arange(row_count, dtype=jnp.int32)
    col_idx = jnp.arange(col_count, dtype=jnp.int32)
    angle = (
        2.0
        * math.pi
        / modulus
        * (row_idx[:, None] * col_idx[None, :] % modulus).astype(jnp.float32)
    )
    return (jnp.cos(angle), jnp.sin(angle))


def complex_section(real_in, imag_in, cosine, sine, form):
    highest = lax.Precision.HIGHEST
    real_out = jnp.einsum(form, cosine, real_in, precision=highest) + jnp.einsum(
        form, sine, imag_in, precision=highest
    )
    imag_out = jnp.einsum(form, cosine, imag_in, precision=highest) - jnp.einsum(
        form, sine, real_in, precision=highest
    )
    return (real_out, imag_out)


def rotate(real_in, imag_in, cosine, sine):
    return (real_in * cosine + imag_in * sine, imag_in * cosine - real_in * sine)


def shards(voltages):
    input_rows = voltages.shape[0]
    local_time = voltages.shape[2]
    chan_count = lax.axis_size("chan")
    spec_local = local_time // NCH
    chan_local = NCH // chan_count
    table = channel_table(NCH)
    samples = (
        voltages.reshape(input_rows, 2, spec_local, NCH)
        .transpose(0, 2, 1, 3)
        .reshape(input_rows * spec_local, 2 * NCH)
    )
    spectra = jnp.dot(samples, table, preferred_element_type=jnp.float32).astype(jnp.bfloat16)
    spectra = spectra.reshape(input_rows, spec_local, 2, NCH)
    turned = lax.all_to_all(spectra, "chan", split_axis=3, concat_axis=1, tiled=True)
    spec_total = turned.shape[1]
    mine = turned.transpose(3, 0, 2, 1).reshape(chan_local, input_rows, 2 * spec_total)
    own_power = jnp.sum(jnp.square(mine.astype(jnp.float32)), axis=2) / spec_total + 1e-06
    own_scale = lax.rsqrt(own_power)
    piece = lax.all_gather(mine, "inp", axis=1, tiled=True)
    half = piece.shape[2] // 2
    rotated = jnp.concatenate([-piece[:, :, half:], piece[:, :, :half]], axis=2)
    numbers = (((2,), (2,)), ((0,), (0,)))
    real_part = lax.dot_general(mine, piece, numbers, preferred_element_type=jnp.float32)
    imag_part = lax.dot_general(mine, rotated, numbers, preferred_element_type=jnp.float32)
    power = jnp.sum(jnp.square(piece.astype(jnp.float32)), axis=2) / spec_total + 1e-06
    scaling = own_scale[:, :, None] * lax.rsqrt(power)[:, None, :] / spec_total
    rho = jnp.stack([real_part * scaling, imag_part * scaling], axis=1).astype(jnp.bfloat16)
    col_local = rho.shape[3] // chan_count
    baseline_count = input_rows * col_local
    arranged = rho.reshape(chan_local, 2, input_rows, chan_count, col_local).transpose(
        3, 0, 1, 2, 4
    )
    arranged = arranged.reshape(chan_count, chan_local, 2, baseline_count)
    regrouped = lax.all_to_all(arranged, "chan", split_axis=0, concat_axis=1, tiled=True)[0].astype(
        jnp.float32
    )
    weighted = regrouped * taper_weights(NCH)[:, None, None]
    first_radix = max((divisor for divisor in range(1, math.isqrt(NCH) + 1) if NCH % divisor == 0))
    second_radix = NCH // first_radix
    field = weighted.reshape(first_radix, second_radix, 2, baseline_count)
    cos_first, sin_first = dft_tables(first_radix, first_radix, first_radix)
    section_real, section_imag = complex_section(
        field[:, :, 0], field[:, :, 1], cos_first, sin_first, "ka,abn->kbn"
    )
    cos_twist, sin_twist = dft_tables(first_radix, second_radix, NCH)
    section_real, section_imag = rotate(
        section_real, section_imag, cos_twist[:, :, None], sin_twist[:, :, None]
    )
    cos_second, sin_second = dft_tables(second_radix, second_radix, second_radix)
    out_real, out_imag = complex_section(
        section_real, section_imag, cos_second, sin_second, "mb,kbn->mkn"
    )
    factor = math.sqrt(spec_total / NCH)
    combined = (
        jnp.stack(
            [out_real.reshape(NCH, baseline_count), out_imag.reshape(NCH, baseline_count)], axis=0
        )
        * factor
    )
    result = combined.transpose(2, 0, 1).reshape(input_rows, col_local, 2, NCH)
    rows_global = lax.axis_index("inp") * input_rows + jnp.arange(input_rows, dtype=jnp.int32)
    cols_global = lax.axis_index("chan") * col_local + jnp.arange(col_local, dtype=jnp.int32)
    same = rows_global[:, None] == cols_global[None, :]
    return jnp.where(same[:, :, None, None], jnp.zeros_like(result), result)


def solution(mesh):
    in_specs = (P("inp", None, "chan"),)
    out_specs = P("inp", "chan", None, None)
    return jax.shard_map(shards, mesh=mesh, in_specs=in_specs, out_specs=out_specs, check_vma=False)
```

profile of v0, /device:TPU:11, one launch (start us, length us, event | category | flops | bytes accessed | tf_op | source)
XLA Modules:
  0.0 1265.4 jit_solution(16086170583561464749)
XLA Ops:
  11.1 7.7 reshape.132
  18.8 15.3 %convert_bitcast_fusion = bf16[2048,1024]{0,1:T(8,128)(2,1)} fusion(bf16[2048,1024]{1,0:T(8,128)(2,1)} %bitcast.72, bf16[512,512]{1,0:T(8,128)(2,1)S(1)} %get-tuple-element.11, bf16[512,512]{1,0:T(8,128)(2,1)S(1)} %get-tuple-element.10, bf16[512,512]{1,0:T(8,128)(2,1)S(1)} %get-tuple-element.9), kind=kOutput, calls=%fused_computation.34 | convolution fusion | flops 4305453056 | bytes 9961472 | tf_op jit(solution)/shard_map/dot_general | solution.py:67
  34.1 6.4 copy.55
  40.5 7.8 reshape.134
  48.3 8.9 copy.56
  57.2 99.0 %all_to_all.27 = bf16[256,8,2,512]{0,1,2,3:T(8,128)(2,1)S(1)} all-to-all(bf16[256,8,2,512]{0,1,2,3:T(8,128)(2,1)} %copy.56), channel_id=1, replica_groups=mesh['chan'=16,'inp'=2] {'chan'}, dimensions={3} | all-to-all | bytes 8388608 | tf_op jit(solution)/shard_map/all_to_all | solution.py:69
  159.9 8.4 copy.59
  168.3 7.6 reshape.135
  179.1 100.9 %all-gather.2.cloned.1.call-done = bf16[32,512,256]{2,1,0:T(8,128)(2,1)} async-done(((bf16[32,256,256]{2,1,0:T(8,128)(2,1)}), bf16[32,512,256]{2,1,0:T(8,128)(2,1)}) %all-gather.2.cloned.1.call-update) | async-done | bytes 8388624 | tf_op jit(solution)/shard_map/all_gather | solution.py:74
  294.6 12.0 copy.61
  306.6 11.8 multiply_convert_fusion.1
  318.4 11.9 copy.60
  330.3 13.8 %maximum_bitcast_fusion = bf16[16,32,2,256,32]{3,4,0,1,2:T(8,128)(2,1)} fusion(bf16[32,1,256,16,32]{2,4,3,0,1:T(8,128)(2,1)} %bitcast.69, bf16[32,1,256,16,32]{2,4,3,0,1:T(8,128)(2,1)} %bitcast.70), kind=kLoop, calls=%fused_computation.5 | loop fusion | flops 8388608 | bytes 33554432 | tf_op jit(solution)/shard_map/transpose | solution.py:85
  344.1 54.0 %copy.62 = bf16[16,32,2,256,32]{4,3,1,2,0:T(8,128)(2,1)} copy(bf16[16,32,2,256,32]{3,4,0,1,2:T(8,128)(2,1)} %maximum_bitcast_fusion) | data formatting | bytes 33554432 | tf_op jit(solution)/shard_map/transpose | solution.py:85
  398.2 81.4 %reshape.136 = bf16[16,32,2,8192]{3,1,2,0:T(8,128)(2,1)} reshape(bf16[16,32,2,256,32]{4,3,1,2,0:T(8,128)(2,1)} %copy.62) | data formatting | bytes 33554432 | tf_op jit(solution)/shard_map/reshape | solution.py:88
  479.6 6.7 all-to-all-start.1
  487.3 361.0 %all-to-all-done.1 = bf16[16,32,2,8192]{3,1,2,0:T(8,128)(2,1)} async-done(((bf16[16,32,2,8192]{3,1,2,0:T(8,128)(2,1)}), bf16[16,32,2,8192]{3,1,2,0:T(8,128)(2,1)}, u32[]{:S(2)}, u32[]{:S(2)}) %all-to-all-start.1) | async-done | bytes 16777248 | tf_op jit(solution)/shard_map/all_to_all | solution.py:89
  848.3 21.9 %convert_multiply_fusion = f32[16,32,2,8192]{3,0,1,2:T(8,128)} fusion(bf16[16,32,2,8192]{3,1,2,0:T(8,128)(2,1)} %all-to-all-done.1, f32[16,32]{0,1:T(8,128)S(1)} %multiply_subtract_fusion.1), kind=kLoop, calls=%fused_computation.2 | loop fusion | flops 16777216 | bytes 50333696 | tf_op jit(solution)/shard_map/mul | solution.py:92
  870.2 21.3 %fusion.2 = f32[16,32,8192]{2,0,1:T(8,128)} fusion(f32[16,32,2,8192]{3,0,1,2:T(8,128)} %convert_multiply_fusion), kind=kOutput, calls=%fused_computation.14 | convolution fusion | flops 805309952 | bytes 33554432 | tf_op jit(solution)/shard_map/ka,abn->kbn/dot_general | solution.py:42
  891.6 21.7 %fusion.1 = f32[16,32,8192]{2,0,1:T(8,128)} fusion(f32[16,32,2,8192]{3,0,1,2:T(8,128)} %convert_multiply_fusion), kind=kOutput, calls=%fused_computation.13 | convolution fusion | flops 805309952 | bytes 33554432 | tf_op jit(solution)/shard_map/ka,abn->kbn/dot_general | solution.py:45
  913.3 23.9 %fusion.13 = f32[16,32,8192]{2,0,1:T(8,128)} fusion(f32[16,32,8192]{2,0,1:T(8,128)} %fusion.2, f32[16,32,2,8192]{3,0,1,2:T(8,128)} %convert_multiply_fusion), kind=kOutput, calls=%fused_computation.25 | convolution fusion | flops 809504256 | bytes 50331648 | tf_op jit(solution)/shard_map/ka,abn->kbn/dot_general | solution.py:42
  937.1 32.0 %multiply_add_fusion = (f32[16,32,8192]{2,0,1:T(8,128)}, f32[16,32,8192]{2,0,1:T(8,128)}) fusion(f32[16,32,8192]{2,0,1:T(8,128)} %fusion.13, f32[16,32]{0,1:T(8,128)S(1)} %get-tuple-element.12, f32[16,32]{0,1:T(8,128)S(1)} %get-tuple-element.13, f32[16,32,8192]{2,0,1:T(8,128)} %fusion.1, f32[16,32,2,8192]{3,0,1,2:T(8,128)} %convert_multiply_fusion), kind=kOutput, calls=%fused_computation.7 | convolution fusion | flops 834670080 | bytes 83890176 | tf_op jit(solution)/shard_map/ka,abn->kbn/dot_general | solution.py:45
  969.1 32.8 %fusion.7 = f32[32,16,8192]{2,0,1:T(8,128)} fusion(f32[16,32,8192]{2,0,1:T(8,128)} %get-tuple-element.6), kind=kOutput, calls=%fused_computation.19 | convolution fusion | flops 1610627072 | bytes 33554432 | tf_op jit(solution)/shard_map/mb,kbn->mkn/dot_general | solution.py:42
  1002.0 33.2 %fusion.5 = f32[32,16,8192]{2,0,1:T(8,128)} fusion(f32[16,32,8192]{2,0,1:T(8,128)} %get-tuple-element.6), kind=kOutput, calls=%fused_computation.17 | convolution fusion | flops 1610627072 | bytes 33554432 | tf_op jit(solution)/shard_map/mb,kbn->mkn/dot_general | solution.py:45
  1035.2 34.7 %fusion.15 = f32[32,16,8192]{2,0,1:T(8,128)} fusion(f32[32,16,8192]{2,0,1:T(8,128)} %fusion.7, f32[16,32,8192]{2,0,1:T(8,128)} %get-tuple-element.5), kind=kOutput, calls=%fused_computation.27 | convolution fusion | flops 1614821376 | bytes 50331648 | tf_op jit(solution)/shard_map/mb,kbn->mkn/dot_general | solution.py:42
  1069.9 17.7 %copy.66 = f32[32,16,8192]{2,1,0:T(8,128)} copy(f32[32,16,8192]{2,0,1:T(8,128)} %fusion.15) | data formatting | bytes 33554432 | tf_op jit(solution)/shard_map/add | solution.py:42
  1087.5 35.4 %fusion.18 = f32[32,16,8192]{2,0,1:T(8,128)} fusion(f32[32,16,8192]{2,0,1:T(8,128)} %fusion.5, f32[16,32,8192]{2,0,1:T(8,128)} %get-tuple-element.5), kind=kOutput, calls=%fused_computation.28 | convolution fusion | flops 1614821376 | bytes 50331648 | tf_op jit(solution)/shard_map/mb,kbn->mkn/dot_general | solution.py:45
  1122.9 15.4 %copy.69 = f32[32,16,8192]{2,1,0:T(8,128)S(1)} copy(f32[32,16,8192]{2,0,1:T(8,128)} %fusion.18) | data formatting | bytes 33554432 | tf_op jit(solution)/shard_map/sub | solution.py:45
  1138.3 11.3 fusion
  1149.7 31.1 %copy.70 = f32[8192,2,512]{2,0,1:T(8,128)} copy(f32[8192,2,512]{0,2,1:T(8,128)} %fusion) | data formatting | bytes 67108864 | tf_op jit(solution)/shard_map/transpose | solution.py:115
  1180.8 22.6 %broadcast_select_fusion = f32[256,32,2,512]{3,1,0,2:T(8,128)} fusion(f32[256,32,2,512]{3,1,0,2:T(8,128)} %bitcast.65, pred[256,32]{1,0:T(8,128)(4,1)S(1)} %copy-done.2), kind=kLoop, calls=%fused_computation.12 | loop fusion | flops 8388608 | bytes 67117056 | tf_op jit(solution)/shard_map/jit(_where)/select_n | solution.py:119
  1203.4 55.0 %copy.71 = f32[256,32,2,512]{3,2,1,0:T(2,128)} copy(f32[256,32,2,512]{3,1,0,2:T(8,128)} %broadcast_select_fusion) | data formatting | bytes 67108864 | tf_op jit(solution)/shard_map/jit(_where)/select_n | solution.py:119
  (22 shorter events, 27.0 us)
Async XLA Ops:
  6.5 273.5 %all-gather.2.cloned.1.call-start = ((), (), s32[]{:S(2)}) async-start(), calls=%async_computation.2 | async-start | bytes 12582912 | tf_op jit(solution)/shard_map/all_gather | solution.py:74
  280.0 9.7 copy-start.1
  479.6 368.7 %all-to-all-start.1 = ((bf16[16,32,2,8192]{3,1,2,0:T(8,128)(2,1)}), bf16[16,32,2,8192]{3,1,2,0:T(8,128)(2,1)}, u32[]{:S(2)}, u32[]{:S(2)}) async-start(bf16[16,32,2,8192]{3,1,2,0:T(8,128)(2,1)} %reshape.136), calls=%async_computation.1 | async-start | bytes 33554432 | tf_op jit(solution)/shard_map/all_to_all | solution.py:89
  1122.9 15.4 %copy-start = (f32[32,16,8192]{2,1,0:T(8,128)S(1)}, f32[32,16,8192]{2,1,0:T(8,128)}, u32[]{:S(2)}) copy-start(f32[32,16,8192]{2,1,0:T(8,128)} %copy.66) | copy-start | bytes 50331652
  1149.7 31.1 %copy-start.2 = (pred[256,32]{1,0:T(8,128)(4,1)S(1)}, pred[256,32]{1,0:T(8,128)(4,1)}, u32[]{:S(2)}) copy-start(pred[256,32]{1,0:T(8,128)(4,1)} %broadcast_compare_fusion) | copy-start | bytes 24580
Sparse Core Ops, SparseCore 0:
  176.1 103.8 all-gather.1
where the time goes:
time: 1280 us; the launch traced here: 1270 us
  waiting for transfers between devices  462 us (36%)
  local copies, waits for them, and re-layouts  329 us (26%)
  matrix products  267 us (21%)
  blocking collectives  99 us (8%)
  other arithmetic  87.9 us (7%)
  between operations  13.8 us (1%)
    all_to_all x1, waiting for transfers between devices, shards(): lax.all_to_all(arranged, 'chan', split_axis=0, concat_axis=1, tiled=True)[0]  361 us
    all_gather x1, waiting for transfers between devices, shards(): piece = lax.all_gather(mine, 'inp', axis=1, tiled=True)  101 us
    all_to_all x1, blocking collectives, shards(): lax.all_to_all(spectra, 'chan', split_axis=3, concat_axis=1, tiled=True)  99 us
    reshape x1, local copies, waits for them, and re-layouts, shards(): arranged = arranged.reshape(chan_count, chan_local, 2, baseline_count)  81.4 us
    dot_general x2, matrix products, complex_section(): jnp.einsum(form, cosine, imag_in, precision=highest)  65.2 us
    dot_general x2, matrix products, complex_section(): jnp.einsum(form, sine, real_in, precision=highest)  57.1 us
    dot_general x2, matrix products, complex_section(): jnp.einsum(form, sine, imag_in, precision=highest)  56.7 us
    dot_general x2, matrix products, complex_section(): jnp.einsum(form, cosine, real_in, precision=highest)  56 us
  transfers between devices with their start and end apart: 2, of which 2 were waited for; matrix products, arithmetic and copies ran while one was open for 0% of the time, Pallas kernels for 0%

commit v1 on v0

v1 whole, which is shorter than its diff:
```python
import functools
import math

import jax
import jax.numpy as jnp
import ml_dtypes
import numpy as np
from jax import lax
from jax.experimental import pallas as pl
from jax.experimental.pallas import tpu as pltpu
from jax.sharding import PartitionSpec as P

NCH = 512
VMEM_LIMIT = 56 * 1024 * 1024


def taper_weights(count):
    position = np.arange(count, dtype=np.float64)
    return 0.5 - 0.5 * np.cos(2.0 * math.pi * (position + 0.5) / count)


def angles(count):
    indices = np.arange(count, dtype=np.int64)
    return 2.0 * math.pi / count * ((indices[:, None] * indices[None, :]) % count)


def channel_table_rows(count):
    angle = angles(count)
    window = taper_weights(count)[:, None] / math.sqrt(count)
    cosine = window * np.cos(angle)
    sine = window * np.sin(angle)
    upper = np.concatenate([cosine, -sine], axis=1)
    lower = np.concatenate([sine, cosine], axis=1)
    table = np.concatenate([upper, lower], axis=0).astype(np.float32)
    return np.ascontiguousarray(table.T).astype(ml_dtypes.bfloat16)


def delay_table(count, spec_total):
    angle = angles(count)
    window = taper_weights(count)[:, None] * math.sqrt(spec_total / count)
    cosine = window * np.cos(angle)
    sine = window * np.sin(angle)
    from_real = np.concatenate([cosine, -sine], axis=1)
    from_imag = np.concatenate([sine, cosine], axis=1)
    return np.stack([from_real, from_imag], axis=1).astype(ml_dtypes.bfloat16)


def channelize(voltages):
    rows, _, local_time = voltages.shape
    spec_local = local_time // NCH
    turned = voltages.transpose(1, 0, 2)
    table = jnp.asarray(channel_table_rows(NCH))
    lines = NCH * 2 * spec_local
    pieces = rows // 128 if rows % 128 == 0 else 1
    width = rows // pieces
    call = pl.pallas_call(
        functools.partial(channelize_kernel, spec_local),
        grid=(pieces, spec_local),
        in_specs=[
            pl.BlockSpec((2 * NCH, 2 * NCH), lambda r, s: (0, 0)),
            pl.BlockSpec((2, width, NCH), lambda r, s: (0, r, s)),
        ],
        out_specs=pl.BlockSpec((lines, width), lambda r, s: (0, r)),
        out_shape=jax.ShapeDtypeStruct((lines, rows), jnp.bfloat16),
        scratch_shapes=[pltpu.VMEM((lines, width), jnp.float32)],
        compiler_params=pltpu.CompilerParams(vmem_limit_bytes=VMEM_LIMIT),
    )
    return call(table, turned)


def channelize_kernel(spec_local, table_ref, volt_ref, out_ref, held):
    step = pl.program_id(1)
    last = (((1,), (1,)), ((), ()))
    depth = 2 * spec_local
    for part in range(2):
        rows = pl.ds(part * NCH, NCH)
        result = lax.dot_general(
            table_ref[rows, :NCH], volt_ref[0], last, preferred_element_type=jnp.float32
        ) + lax.dot_general(
            table_ref[rows, NCH:], volt_ref[1], last, preferred_element_type=jnp.float32
        )
        held[pl.ds(part * spec_local + step, NCH, stride=depth), :] = result

    @pl.when(step == spec_local - 1)
    def _():
        out_ref[...] = held[...].astype(jnp.bfloat16)


def visibility_kernel(spec_total, count, half_depth, mine_ref, piece_ref, out_ref, held):
    step = pl.program_id(1)
    sources, _, depth, rows = mine_ref.shape
    mine = mine_ref[:, 0]
    turned = jnp.concatenate([mine[:, half_depth:], -mine[:, :half_depth]], axis=1)
    mine = mine.reshape(sources * depth, rows)
    turned = turned.reshape(sources * depth, rows)
    piece = piece_ref[0, :, 0].reshape(sources * depth, rows)

    def scale(block):
        wide = block.astype(jnp.float32)
        power = jnp.sum(wide * wide, axis=0, keepdims=True) / spec_total + 1e-06
        return lax.rsqrt(power)

    own = scale(mine) / spec_total
    other = jnp.transpose(jnp.broadcast_to(scale(piece), (8, rows)))[:, :1]
    numbers = (((0,), (0,)), ((), ()))
    for part, block in enumerate((mine, turned)):
        value = lax.dot_general(piece, block, numbers, preferred_element_type=jnp.float32)
        value = value * (other * own)
        cols = value.shape[1]
        for start in range(0, cols, min(128, cols)):
            wide = min(128, cols)
            held[part * (cols // wide) + start // wide, pl.ds(step, rows, stride=count), :] = value[
                :, start : start + wide
            ]

    @pl.when(step == count - 1)
    def _():
        wide = held.shape[2]
        for tile in range(held.shape[0]):
            out_ref[:, tile * wide : (tile + 1) * wide] = held[tile].astype(jnp.bfloat16)


def visibilities(mine, gathered, spec_total):
    inputs = gathered.shape[0]
    sources, count, depth, rows = mine.shape
    wide = min(128, rows)
    call = pl.pallas_call(
        functools.partial(visibility_kernel, spec_total, count, depth // 2),
        grid=(inputs, count),
        in_specs=[
            pl.BlockSpec((sources, 1, depth, rows), lambda h, c: (0, c, 0, 0)),
            pl.BlockSpec((1, sources, 1, depth, rows), lambda h, c: (h, 0, c, 0, 0)),
        ],
        out_specs=pl.BlockSpec((rows * count, 2 * rows), lambda h, c: (h, 0)),
        out_shape=jax.ShapeDtypeStruct((inputs * rows * count, 2 * rows), jnp.bfloat16),
        scratch_shapes=[pltpu.VMEM((2 * rows // wide, rows * count, wide), jnp.float32)],
        compiler_params=pltpu.CompilerParams(vmem_limit_bytes=VMEM_LIMIT),
    )
    return call(mine, gathered)


def delay_kernel(chunks, rows, offset_ref, table_ref, *refs):
    blocks, out_ref = refs[:chunks], refs[chunks]
    numbers = (((0,), (0,)), ((), ()))
    total = None
    for chunk in range(chunks):
        sources, _, count, wide = blocks[chunk].shape
        block = blocks[chunk][:, 0].reshape(sources * count, wide)
        for part in range(2):
            term = lax.dot_general(
                block[:, part * rows : (part + 1) * rows],
                table_ref[chunk, part],
                numbers,
                preferred_element_type=jnp.float32,
            )
            total = term if total is None else total + term
    column = offset_ref[0] + pl.program_id(0)
    same = lax.broadcasted_iota(jnp.int32, (rows, 1), 0) == column
    total = jnp.where(same, 0.0, total)
    for part in range(2):
        out_ref[:, 0, part, :] = total[:, part * NCH : (part + 1) * NCH]


def delay_spectra(received, table, offset, rows):
    chunks = len(received)
    sources, cols, count, wide = received[0].shape
    call = pl.pallas_call(
        functools.partial(delay_kernel, chunks, rows),
        grid=(cols,),
        in_specs=[
            pl.BlockSpec(memory_space=pltpu.SMEM),
            pl.BlockSpec(table.shape, lambda j: (0, 0, 0, 0)),
        ]
        + [pl.BlockSpec((sources, 1, count, wide), lambda j: (0, j, 0, 0))] * chunks,
        out_specs=pl.BlockSpec((rows, 1, 2, NCH), lambda j: (0, j, 0, 0)),
        out_shape=jax.ShapeDtypeStruct((rows, cols, 2, NCH), jnp.float32),
        compiler_params=pltpu.CompilerParams(vmem_limit_bytes=VMEM_LIMIT),
    )
    return call(offset, table, *received)


def shards(voltages):
    rows, _, local_time = voltages.shape
    chan_count = lax.axis_size("chan")
    inp_count = lax.axis_size("inp")
    spec_local = local_time // NCH
    spec_total = spec_local * chan_count
    chan_local = NCH // chan_count
    col_local = rows * inp_count // chan_count
    depth = 2 * spec_local
    count = chan_local // 2 if chan_local % 32 == 0 else chan_local
    chunks = chan_local // count

    spectra = channelize(voltages).reshape(chan_count, chunks, count, depth, rows)
    mine = []
    for chunk in range(chunks):
        mine.append(lax.all_to_all(spectra[:, chunk], "chan", split_axis=0, concat_axis=0, tiled=True))
    received = []
    for chunk in range(chunks):
        gathered = lax.all_gather(mine[chunk], "inp", axis=0, tiled=False)
        rho = visibilities(mine[chunk], gathered, spec_total)
        rho = rho.reshape(chan_count, col_local, count, 2 * rows)
        received.append(lax.all_to_all(rho, "chan", split_axis=0, concat_axis=0, tiled=True))

    table = delay_table(NCH, spec_total)
    table = table.reshape(chan_count, chunks, count, 2, 2 * NCH).transpose(1, 3, 0, 2, 4)
    table = jnp.asarray(np.ascontiguousarray(table).reshape(chunks, 2, chan_count * count, 2 * NCH))
    offset = lax.axis_index("chan") * col_local - lax.axis_index("inp") * rows
    return delay_spectra(received, table, offset.astype(jnp.int32).reshape(1), rows)


def solution(mesh):
    in_specs = (P("inp", None, "chan"),)
    out_specs = P("inp", "chan", None, None)
    return jax.shard_map(shards, mesh=mesh, in_specs=in_specs, out_specs=out_specs, check_vma=False)
```

time: 1280 us -> 601 us (0.47)
  local copies, waits for them, and re-layouts: 329 us -> 12.3 us
  matrix products: 267 us -> 0 us
  Pallas kernels: 0 us -> 116 us
  other arithmetic: 87.9 us -> 0 us
  waiting for transfers between devices: 462 us -> 387 us
  blocking collectives: 99 us -> 53.8 us
    dot_general x11 -> x0, matrix products: 267 us -> none  [the longest x2 65.2 us: complex_section(): jnp.einsum(form, cosine, imag_in, precision=highest)]
    pallas_call x0 -> x4, Pallas kernels: none -> 116 us  [the longest x2 58.6 us: visibilities(): return call(mine, gathered)]
    reshape x5 -> x0, local copies, waits for them, and re-layouts: 113 us -> none  [the longest x1 81.4 us: shards(): arranged = arranged.reshape(chan_count, chan_local, 2, baseline_count)]
    transpose x3 -> x0, local copies, waits for them, and re-layouts: 93.5 us -> none  [the longest x1 54 us: shards(): rho.reshape(chan_local, 2, input_rows, chan_count, col_local)]
    all_to_all x1 -> x3, waiting for transfers between devices: 361 us -> 277 us  [the longest x2 277 us: shards(): lax.all_to_all(rho, 'chan', split_axis=0, concat_axis=0, tiled=True)]
    select_n x1 -> x0, local copies, waits for them, and re-layouts: 55 us -> none  [shards(): return jnp.where(same[:, :, None, None], jnp.zeros_like(result), result)]
    all_to_all x1, blocking collectives: 99 us -> 53.8 us  [shards(): lax.all_to_all(spectra[:, chunk], 'chan', split_axis=0, concat_axis=0, ti...]
    transpose x2 -> x0, other arithmetic: 25.1 us -> none  [the longest x1 13.8 us: shards(): rho.reshape(chan_local, 2, input_rows, chan_count, col_local)]
  transfers between devices with their start and end apart: 2 -> 5, of which waited for: 2 -> 4; matrix products, arithmetic and copies ran while one was open for 0% -> 0% of each run, Pallas kernels for 0% -> 10%
where the time goes in v1:
time: 601 us; the launch traced here: 599 us
  waiting for transfers between devices  387 us (64%)
  Pallas kernels  116 us (19%)
  blocking collectives  53.8 us (9%)
  starting transfers between devices  16.5 us (3%)
  between operations  13.4 us (2%)
  local copies, waits for them, and re-layouts  12.3 us (2%)
    all_to_all x2, waiting for transfers between devices, shards(): lax.all_to_all(rho, 'chan', split_axis=0, concat_axis=0, tiled=True)  277 us
    all_gather x2, waiting for transfers between devices, shards(): gathered = lax.all_gather(mine[chunk], 'inp', axis=0, tiled=False)  110 us
    pallas_call x2, Pallas kernels, visibilities(): return call(mine, gathered)  58.6 us
    all_to_all x1, blocking collectives, shards(): lax.all_to_all(spectra[:, chunk], 'chan', split_axis=0, concat_axis=0, ti...  53.8 us
    pallas_call x1, Pallas kernels, delay_spectra(): return call(offset, table, *received)  39.4 us
    pallas_call x1, Pallas kernels, channelize(): return call(table, turned)  17.9 us
  transfers between devices with their start and end apart: 5, of which 4 were waited for; matrix products, arithmetic and copies ran while one was open for 0% of the time, Pallas kernels for 10%

profile of v1, /device:TPU:11, one launch (start us, length us, event | category | flops | bytes accessed | tf_op | source)
XLA Modules:
  0.0 598.7 jit_solution(17919127742780283861)
XLA Ops:
  6.5 0.0 all-gather.5.cloned.1.call-start
  6.5 7.1 %copy.14 = bf16[256,2,4096]{2,0,1:T(8,128)(2,1)} copy(bf16[256,2,4096]{2,1,0:T(2,128)(2,1)} %param.3) | data formatting | bytes 8388608 | tf_op args[0]
  13.6 17.9 %shard_map.37 = bf16[8192,256]{1,0:T(8,128)(2,1)} custom-call(bf16[1024,1024]{1,0:T(8,128)(2,1)} %constant.16.clone.table_ref, bf16[2,256,4096]{2,1,0:T(8,128)(2,1)} %bitcast.20), custom_call_target="tpu_custom_call" | custom-call | tf_op jit(solution)/shard_map/pallas_call | solution.py:68
  31.6 3.9 slice_bitcast_fusion
  35.5 53.8 %all_to_all.20.mine_ref = bf16[16,16,16,256]{3,2,1,0:T(8,128)(2,1)} all-to-all(bf16[16,16,16,256]{3,2,1,0:T(8,128)(2,1)S(1)} %get-tuple-element.6), channel_id=1, replica_groups=mesh['chan'=16,'inp'=2] {'chan'}, dimensions={0} | all-to-all | bytes 4194304 | tf_op jit(solution)/shard_map/all_to_all | solution.py:197
  89.2 0.0 all-gather.5.cloned.1.call-update
  89.2 5.1 all-to-all-start.2
  94.4 51.5 %all-gather.5.cloned.1.call-done = bf16[32,16,16,256]{3,2,1,0:T(8,128)(2,1)} async-done(((bf16[16,16,16,256]{3,2,1,0:T(8,128)(2,1)}), bf16[32,16,16,256]{3,2,1,0:T(8,128)(2,1)}) %all-gather.5.cloned.1.call-update) | async-done | bytes 4194320 | tf_op jit(solution)/shard_map/all_gather | solution.py:200
  145.8 29.4 %shard_map.38 = bf16[8192,512]{1,0:T(8,128)(2,1)} custom-call(bf16[16,16,16,256]{3,2,1,0:T(8,128)(2,1)} %all_to_all.20.mine_ref, bf16[2,16,16,16,256]{4,3,2,1,0:T(8,128)(2,1)} %bitcast.21), custom_call_target="tpu_custom_call" | custom-call | tf_op jit(solution)/shard_map/pallas_call | solution.py:139
  175.2 0.0 all-to-all-done.2.mine_ref
  175.2 0.0 copy-start
  175.2 1.3 copy-done
  176.5 6.4 %all-to-all-start.1 = ((bf16[16,32,16,512]{3,2,1,0:T(8,128)(2,1)}), bf16[16,32,16,512]{3,2,1,0:T(8,128)(2,1)}, u32[]{:S(2)}, u32[]{:S(2)}) async-start(bf16[16,32,16,512]{3,2,1,0:T(8,128)(2,1)} %bitcast.18), calls=%async_computation.1 | async-start | bytes 16777216 | tf_op jit(solution)/shard_map/all_to_all | solution.py:203
  182.9 0.0 all-gather.7.cloned.1.call-start
  183.0 0.7 all-gather.7.cloned.1.call-update
  183.7 58.1 %all-gather.7.cloned.1.call-done = bf16[32,16,16,256]{3,2,1,0:T(8,128)(2,1)} async-done(((bf16[16,16,16,256]{3,2,1,0:T(8,128)(2,1)}), bf16[32,16,16,256]{3,2,1,0:T(8,128)(2,1)}) %all-gather.7.cloned.1.call-update) | async-done | bytes 4194320 | tf_op jit(solution)/shard_map/all_gather | solution.py:200
  241.7 29.2 %shard_map.39 = bf16[8192,512]{1,0:T(8,128)(2,1)} custom-call(bf16[16,16,16,256]{3,2,1,0:T(8,128)(2,1)} %copy-done, bf16[2,16,16,16,256]{4,3,2,1,0:T(8,128)(2,1)} %bitcast.22), custom_call_target="tpu_custom_call" | custom-call | tf_op jit(solution)/shard_map/pallas_call | solution.py:139
  270.9 94.3 %all-to-all-done.1.refs_0_ = bf16[16,32,16,512]{3,2,1,0:T(8,128)(2,1)} async-done(((bf16[16,32,16,512]{3,2,1,0:T(8,128)(2,1)}), bf16[16,32,16,512]{3,2,1,0:T(8,128)(2,1)}, u32[]{:S(2)}, u32[]{:S(2)}) %all-to-all-start.1) | async-done | bytes 8388640 | tf_op jit(solution)/shard_map/all_to_all | solution.py:203
  365.3 4.9 all-to-all-start.3
  370.2 182.3 %all-to-all-done.3.refs_1_ = bf16[16,32,16,512]{3,2,1,0:T(8,128)(2,1)} async-done(((bf16[16,32,16,512]{3,2,1,0:T(8,128)(2,1)}), bf16[16,32,16,512]{3,2,1,0:T(8,128)(2,1)}, u32[]{:S(2)}, u32[]{:S(2)}) %all-to-all-start.3) | async-done | bytes 8388640 | tf_op jit(solution)/shard_map/all_to_all | solution.py:203
  552.5 39.4 %shard_map.40 = f32[256,32,2,512]{3,2,1,0:T(2,128)} custom-call(s32[1]{0:T(128)} %bitcast.offset_ref, bf16[2,2,256,1024]{3,2,1,0:T(8,128)(2,1)} %constant.17.clone.table_ref, bf16[16,32,16,512]{3,2,1,0:T(8,128)(2,1)} %all-to-all-done.1.refs_0_, bf16[16,32,16,512]{3,2,1,0:T(8,128)(2,1)} %all-to-all-done.3.refs_1_), custom_call_target="tpu_custom_call" | custom-call | tf_op jit(solution)/shard_map/pallas_call | solution.py:179
Async XLA Ops:
  6.5 139.3 %all-gather.5.cloned.1.call-start = ((), (), s32[]{:S(2)}) async-start(), calls=%async_computation.4 | async-start | bytes 6291456 | tf_op jit(solution)/shard_map/all_gather | solution.py:200
  89.2 86.0 %all-to-all-start.2 = ((bf16[16,16,16,256]{3,2,1,0:T(8,128)(2,1)}), bf16[16,16,16,256]{3,2,1,0:T(8,128)(2,1)S(1)}, u32[]{:S(2)}, u32[]{:S(2)}) async-start(bf16[16,16,16,256]{3,2,1,0:T(8,128)(2,1)} %get-tuple-element.5), calls=%async_computation.2 | async-start | bytes 4194304 | tf_op jit(solution)/shard_map/all_to_all | solution.py:197
  175.2 1.3 copy-start
  176.5 188.7 %all-to-all-start.1 = ((bf16[16,32,16,512]{3,2,1,0:T(8,128)(2,1)}), bf16[16,32,16,512]{3,2,1,0:T(8,128)(2,1)}, u32[]{:S(2)}, u32[]{:S(2)}) async-start(bf16[16,32,16,512]{3,2,1,0:T(8,128)(2,1)} %bitcast.18), calls=%async_computation.1 | async-start | bytes 16777216 | tf_op jit(solution)/shard_map/all_to_all | solution.py:203
  182.9 58.8 %all-gather.7.cloned.1.call-start = ((), (), s32[]{:S(2)}) async-start(), calls=%async_computation.5 | async-start | bytes 6291456 | tf_op jit(solution)/shard_map/all_gather | solution.py:200
  365.3 187.3 %all-to-all-start.3 = ((bf16[16,32,16,512]{3,2,1,0:T(8,128)(2,1)}), bf16[16,32,16,512]{3,2,1,0:T(8,128)(2,1)}, u32[]{:S(2)}, u32[]{:S(2)}) async-start(bf16[16,32,16,512]{3,2,1,0:T(8,128)(2,1)} %bitcast.17), calls=%async_computation.3 | async-start | bytes 16777216 | tf_op jit(solution)/shard_map/all_to_all | solution.py:203
Sparse Core Ops, SparseCore 0:
  89.3 56.4 all-gather.4
  185.3 56.3 all-gather.6

commit v2 on v1

--- a/solution.py
+++ b/solution.py
@@ -162,8 +162,7 @@
 
 
 def delay_spectra(received, table, offset, rows):
-    chunks = len(received)
-    sources, cols, count, wide = received[0].shape
+    sources, chunks, cols, count, wide = received.shape
     call = pl.pallas_call(
         functools.partial(delay_kernel, chunks, rows),
         grid=(cols,),
@@ -171,12 +170,15 @@
             pl.BlockSpec(memory_space=pltpu.SMEM),
             pl.BlockSpec(table.shape, lambda j: (0, 0, 0, 0)),
         ]
-        + [pl.BlockSpec((sources, 1, count, wide), lambda j: (0, j, 0, 0))] * chunks,
+        + [
+            pl.BlockSpec((sources, None, 1, count, wide), lambda j, chunk=chunk: (0, chunk, j, 0, 0))
+            for chunk in range(chunks)
+        ],
         out_specs=pl.BlockSpec((rows, 1, 2, NCH), lambda j: (0, j, 0, 0)),
         out_shape=jax.ShapeDtypeStruct((rows, cols, 2, NCH), jnp.float32),
         compiler_params=pltpu.CompilerParams(vmem_limit_bytes=VMEM_LIMIT),
     )
-    return call(offset, table, *received)
+    return call(offset, table, *([received] * chunks))
 
 
 def shards(voltages):
@@ -195,12 +197,13 @@
     mine = []
     for chunk in range(chunks):
         mine.append(lax.all_to_all(spectra[:, chunk], "chan", split_axis=0, concat_axis=0, tiled=True))
-    received = []
+    rhos = []
     for chunk in range(chunks):
         gathered = lax.all_gather(mine[chunk], "inp", axis=0, tiled=False)
         rho = visibilities(mine[chunk], gathered, spec_total)
-        rho = rho.reshape(chan_count, col_local, count, 2 * rows)
-        received.append(lax.all_to_all(rho, "chan", split_axis=0, concat_axis=0, tiled=True))
+        rhos.append(rho.reshape(chan_count, col_local, count, 2 * rows))
+    rho = jnp.stack(rhos, axis=1)
+    received = lax.all_to_all(rho, "chan", split_axis=0, concat_axis=0, tiled=True)
 
     table = delay_table(NCH, spec_total)
     table = table.reshape(chan_count, chunks, count, 2, 2 * NCH).transpose(1, 3, 0, 2, 4)

time: 601 us -> 663 us (1.10)
  blocking collectives: 53.8 us -> 106 us
  other arithmetic: 0 us -> 13.8 us
  starting transfers between devices: 16.5 us -> 6.6 us
  waiting for transfers between devices: 387 us -> 395 us
    all_to_all x2 -> x1, waiting for transfers between devices: 277 us -> 362 us  [shards(): lax.all_to_all(rho, 'chan', split_axis=0, concat_axis=0, tiled=True)]
    all_gather x2, waiting for transfers between devices: 110 us -> 32.7 us  [shards(): gathered = lax.all_gather(mine[chunk], 'inp', axis=0, tiled=False)]
    all_to_all x1 -> x2, blocking collectives: 53.8 us -> 106 us  [shards(): lax.all_to_all(spectra[:, chunk], 'chan', split_axis=0, concat_axis=0, ti...]
    another operation x0 -> x1, other arithmetic: none -> 13.8 us  [shards(): rho = jnp.stack(rhos, axis=1)]
  transfers between devices with their start and end apart: 5 -> 3, of which waited for: 4 -> 3; matrix products, arithmetic and copies ran while one was open for 0% -> 0% of each run, Pallas kernels for 10% -> 4%
where the time goes in v2:
time: 663 us; the launch traced here: 661 us
  waiting for transfers between devices  395 us (60%)
  Pallas kernels  116 us (17%)
  blocking collectives  106 us (16%)
  other arithmetic  13.8 us (2%)
  between operations  13.4 us (2%)
  local copies, waits for them, and re-layouts  9.63 us (1%)
    all_to_all x1, waiting for transfers between devices, shards(): lax.all_to_all(rho, 'chan', split_axis=0, concat_axis=0, tiled=True)  362 us
    all_to_all x2, blocking collectives, shards(): lax.all_to_all(spectra[:, chunk], 'chan', split_axis=0, concat_axis=0, ti...  106 us
    pallas_call x2, Pallas kernels, visibilities(): return call(mine, gathered)  58.6 us
    pallas_call x1, Pallas kernels, delay_spectra(): return call(offset, table, *[received] * chunks)  39.4 us
    all_gather x2, waiting for transfers between devices, shards(): gathered = lax.all_gather(mine[chunk], 'inp', axis=0, tiled=False)  32.7 us
    pallas_call x1, Pallas kernels, channelize(): return call(table, turned)  17.9 us
    another operation x1, other arithmetic, shards(): rho = jnp.stack(rhos, axis=1)  13.8 us
  transfers between devices with their start and end apart: 3, of which 3 were waited for; matrix products, arithmetic and copies ran while one was open for 0% of the time, Pallas kernels for 4%

profile of v2, /device:TPU:11, one launch (start us, length us, event | category | flops | bytes accessed | tf_op | source)
XLA Modules:
  0.0 660.6 jit_solution(12606672447726450408)
XLA Ops:
  6.5 0.0 all-gather.7.cloned.1.call-start
  6.5 7.1 %copy.14 = bf16[256,2,4096]{2,0,1:T(8,128)(2,1)} copy(bf16[256,2,4096]{2,1,0:T(2,128)(2,1)} %param.3) | data formatting | bytes 8388608 | tf_op args[0]
  13.6 17.9 %shard_map.37 = bf16[8192,256]{1,0:T(8,128)(2,1)} custom-call(bf16[1024,1024]{1,0:T(8,128)(2,1)} %constant.16.clone.table_ref, bf16[2,256,4096]{2,1,0:T(8,128)(2,1)} %bitcast.20), custom_call_target="tpu_custom_call" | custom-call | tf_op jit(solution)/shard_map/pallas_call | solution.py:68
  31.5 2.5 slice_bitcast_fusion.1
  34.1 53.8 %all_to_all.15.mine_ref = bf16[16,16,16,256]{3,2,1,0:T(8,128)(2,1)} all-to-all(bf16[16,16,16,256]{3,2,1,0:T(8,128)(2,1)S(1)} %get-tuple-element.6), channel_id=1, replica_groups=mesh['chan'=16,'inp'=2] {'chan'}, dimensions={0} | all-to-all | bytes 4194304 | tf_op jit(solution)/shard_map/all_to_all | solution.py:199
  87.8 0.0 all-gather.7.cloned.1.call-update
  87.9 0.0 all-gather.5.cloned.1.call-start
  87.9 52.6 %all_to_all.16.mine_ref = bf16[16,16,16,256]{3,2,1,0:T(8,128)(2,1)} all-to-all(bf16[16,16,16,256]{3,2,1,0:T(8,128)(2,1)S(1)} %get-tuple-element.5), channel_id=1, replica_groups=mesh['chan'=16,'inp'=2] {'chan'}, dimensions={0} | all-to-all | bytes 4194304 | tf_op jit(solution)/shard_map/all_to_all | solution.py:199
  140.5 0.0 all-gather.5.cloned.1.call-update
  140.6 3.9 all-gather.7.cloned.1.call-done
  144.5 29.4 %shard_map.39 = bf16[8192,512]{1,0:T(8,128)(2,1)} custom-call(bf16[16,16,16,256]{3,2,1,0:T(8,128)(2,1)} %all_to_all.15.mine_ref, bf16[2,16,16,16,256]{4,3,2,1,0:T(8,128)(2,1)} %bitcast.21), custom_call_target="tpu_custom_call" | custom-call | tf_op jit(solution)/shard_map/pallas_call | solution.py:139
  173.9 28.8 %all-gather.5.cloned.1.call-done = bf16[32,16,16,256]{3,2,1,0:T(8,128)(2,1)} async-done(((bf16[16,16,16,256]{3,2,1,0:T(8,128)(2,1)}), bf16[32,16,16,256]{3,2,1,0:T(8,128)(2,1)}) %all-gather.5.cloned.1.call-update) | async-done | bytes 4194320 | tf_op jit(solution)/shard_map/all_gather | solution.py:202
  202.7 29.2 %shard_map.38 = bf16[8192,512]{1,0:T(8,128)(2,1)} custom-call(bf16[16,16,16,256]{3,2,1,0:T(8,128)(2,1)} %all_to_all.16.mine_ref, bf16[2,16,16,16,256]{4,3,2,1,0:T(8,128)(2,1)} %bitcast.22), custom_call_target="tpu_custom_call" | custom-call | tf_op jit(solution)/shard_map/pallas_call | solution.py:139
  231.9 13.8 %pad_maximum_fusion = bf16[16,2,32,16,512]{4,3,2,1,0:T(8,128)(2,1)} fusion(bf16[16,1,32,16,512]{4,3,2,1,0:T(8,128)(2,1)} %bitcast.17, bf16[16,1,32,16,512]{4,3,2,1,0:T(8,128)(2,1)} %bitcast.18), kind=kLoop, calls=%fused_computation | loop fusion | flops 8388608 | bytes 33554432 | tf_op jit(solution)/shard_map/stack | solution.py:205
  245.7 6.6 all-to-all-start.2
  252.3 362.1 %all-to-all-done.2.refs_0_.refs_1_ = bf16[16,2,32,16,512]{4,3,2,1,0:T(8,128)(2,1)} async-done(((bf16[16,2,32,16,512]{4,3,2,1,0:T(8,128)(2,1)}), bf16[16,2,32,16,512]{4,3,2,1,0:T(8,128)(2,1)}, u32[]{:S(2)}, u32[]{:S(2)}) %all-to-all-start.2) | async-done | bytes 16777248 | tf_op jit(solution)/shard_map/all_to_all | solution.py:206
  614.4 39.4 %shard_map.40 = f32[256,32,2,512]{3,2,1,0:T(2,128)} custom-call(s32[1]{0:T(128)} %bitcast.offset_ref, bf16[2,2,256,1024]{3,2,1,0:T(8,128)(2,1)} %constant.17.clone.table_ref, bf16[16,2,32,16,512]{4,3,2,1,0:T(8,128)(2,1)} %all-to-all-done.2.refs_0_.refs_1_, bf16[16,2,32,16,512]{4,3,2,1,0:T(8,128)(2,1)} %all-to-all-done.2.refs_0_.refs_1_), custom_call_target="tpu_custom_call" | custom-call | tf_op jit(solution)/shard_map/pallas_call | solution.py:181
Async XLA Ops:
  6.5 137.9 %all-gather.7.cloned.1.call-start = ((), (), s32[]{:S(2)}) async-start(), calls=%async_computation.4 | async-start | bytes 6291456 | tf_op jit(solution)/shard_map/all_gather | solution.py:202
  87.9 114.8 %all-gather.5.cloned.1.call-start = ((), (), s32[]{:S(2)}) async-start(), calls=%async_computation.3 | async-start | bytes 6291456 | tf_op jit(solution)/shard_map/all_gather | solution.py:202
  245.7 368.7 %all-to-all-start.2 = ((bf16[16,2,32,16,512]{4,3,2,1,0:T(8,128)(2,1)}), bf16[16,2,32,16,512]{4,3,2,1,0:T(8,128)(2,1)}, u32[]{:S(2)}, u32[]{:S(2)}) async-start(bf16[16,2,32,16,512]{4,3,2,1,0:T(8,128)(2,1)} %pad_maximum_fusion), calls=%async_computation.2 | async-start | bytes 33554432 | tf_op jit(solution)/shard_map/all_to_all | solution.py:206
Sparse Core Ops, SparseCore 0:
  88.0 56.4 all-gather.6
  146.0 56.6 all-gather.4
